TPU v7x, 32 devices: a whole 2x2x4 slice. The times are simulated.
32 devices in a mesh: row: 8 (over z, core), col: 4 (over y, x).
Axes of the slice: x: 2, y: 2, z: 4, core: 2. Of those that a mesh axis runs over, the one named last changes fastest.
Arguments:
- trailing: bfloat16 [6144, 3072], P('row', 'col'), may hold values from -6 to 6
- offdiagonal_panel_rows: bfloat16 [2, 6144, 512], P(None, ('row', 'col')), may hold values from -3 to 3
- pivot_diagonal_blocks: bfloat16 [2, 512, 512], replicated, may hold values from -3 to 14, as said below
- coupling: bfloat16 [512, 512], replicated, may hold values from -0.3314563 to 0.3314563, as said below
- pattern: int32 [2, 48], replicated, may hold values 0 or 1
- block_slot_lookup: int32 [48], replicated, may hold values from 0 to 47, each once
- elimination_sequence: int32 [2], replicated, may hold values from 0 to 1, each once
Outputs:
- updated: bfloat16 [6144, 3072], P('row', 'col')
- factor: bfloat16 [2, 6144, 512], P(None, ('row', 'col'))
Inputs may be any that keep to these rules, and one draw needn't show every extreme that they name: `pivot_diagonal_blocks`: each diagonal block is symmetric positive definite. `coupling`: pivot_diagonal_blocks[b] - link link^T is positive definite. `elimination_sequence`: a permutation of the two panel indices.
All inputs are finite; a program needn't handle non-finite values.
Results may differ from a plain program's by a relative error of at most 0.0055.
Values may be sent and summed in bfloat16 or wider, within the bound.
A program may use at most 64 MiB of HBM per device.

v0:
```python
import jax
import jax.numpy as jnp
from jax import lax
from jax.sharding import PartitionSpec as P

B = 128


def from_root(value, axis, source):
    kept = jnp.where(lax.axis_index(axis) == source, value, 0).astype(value.dtype)
    return lax.psum(kept, axis)


def solve_right(rhs, lower_factor):
    return jax.scipy.linalg.solve_triangular(lower_factor, rhs.T, lower=True).T


def product_rows(left, right):
    return lax.dot_general(
        left, right, (((1,), (1,)), ((), ())), preferred_element_type=jnp.float32
    )


def local(
    trailing,
    offdiagonal_panel_rows,
    pivot_diagonal_blocks,
    coupling,
    pattern,
    block_slot_lookup,
    elimination_sequence,
):
    width = offdiagonal_panel_rows.shape[1]
    col_count = lax.axis_size("col")
    row_index = lax.axis_index("row")
    col_index = lax.axis_index("col")
    first_row = (row_index * col_count + col_index) * width
    slots = (first_row + jnp.arange(width, dtype=jnp.int32)) // B
    total_blocks = block_slot_lookup.shape[0]
    every_block = jnp.arange(total_blocks, dtype=jnp.int32)
    slot_hit = (slots[:, None] == every_block[None, :]).astype(jnp.int32)
    global_block = jnp.sum(slot_hit * block_slot_lookup[None, :], axis=1)
    block_hit = (global_block[:, None] == every_block[None, :]).astype(jnp.int32)
    keep_mask = jnp.sum(pattern[:, None, :] * block_hit[None], axis=2)
    masked = offdiagonal_panel_rows * keep_mask[:, :, None].astype(jnp.bfloat16)
    exchanged_panels = elimination_sequence[0] == 1
    sorted_panels = jnp.where(exchanged_panels, masked[::-1], masked)
    diagonals = pivot_diagonal_blocks.astype(jnp.float32)
    diagonals = jnp.where(exchanged_panels, diagonals[::-1], diagonals)
    couple = coupling.astype(jnp.float32)
    kmat = jnp.where(exchanged_panels, couple.T, couple)
    first_factor = jnp.linalg.cholesky(diagonals[0])
    link = solve_right(kmat, first_factor).astype(jnp.bfloat16)
    shrunk = diagonals[1] - product_rows(link, link)
    second_factor = jnp.linalg.cholesky(shrunk)
    whole_rows = lax.all_gather(sorted_panels, "col", axis=1, tiled=True)
    leading_rows = solve_right(whole_rows[0].astype(jnp.float32), first_factor).astype(jnp.bfloat16)
    updated_rows = whole_rows[1].astype(jnp.float32) - product_rows(leading_rows, link)
    second_rows = solve_right(updated_rows, second_factor).astype(jnp.bfloat16)
    row_factor = jnp.stack([leading_rows, second_rows])
    local_factor = lax.dynamic_slice_in_dim(row_factor, col_index * width, width, 1)
    col_factor = from_root(row_factor, "row", col_index)
    result = trailing.astype(jnp.float32)
    left_operand = jnp.concatenate([row_factor[0], row_factor[1]], axis=1)
    right_side = jnp.concatenate([col_factor[0], col_factor[1]], axis=1)
    result = result - product_rows(left_operand, right_side)
    factor = jnp.where(exchanged_panels, local_factor[::-1], local_factor)
    return (result.astype(jnp.bfloat16), factor)


def solution(mesh):
    return jax.shard_map(
        local,
        mesh=mesh,
        in_specs=(P("row", "col"), P(None, ("row", "col"), None), P(), P(), P(), P(), P()),
        out_specs=(P("row", "col"), P(None, ("row", "col"), None)),
        check_vma=False,
    )
```

profile of v0, /device:TPU:0, one launch (start us, length us, event | category | flops | bytes accessed | tf_op | source)
XLA Modules:
  0.0 418.6 jit_solution(8209657463598200847)
XLA Ops:
  7.2 0.7 select_reduce_fusion.8
  8.0 0.8 multiply_reduce_fusion
  8.8 1.2 copy.28
  10.8 1.1 copy.29
  12.7 1.1 fusion.19
  15.3 1.0 slice_bitcast_fusion.1
  16.3 1.6 copy.27
  18.1 1.0 copy-done.4
  19.1 11.7 %cholesky.286 = f32[128,128]{1,0:T(8,128)S(1)} custom-call(f32[128,128]{1,0:T(8,128)S(1)} %cholesky.426), custom_call_target="Cholesky" | custom-call | tf_op jit(solution)/shard_map/jit(cholesky)/cholesky | solution.py:52
  30.8 9.8 %custom-call.32 = f32[1,128,128]{1,2,0:T(8,128)S(1)} custom-call(f32[1,128,128]{2,1,0:T(8,128)S(1)} %get-tuple-element.81), custom_call_target="InvertDiagBlocksLowerTriangular" | custom-call | tf_op jit(solution)/shard_map/jit(cholesky)/cholesky | solution.py:52
  40.8 1.2 constant_dynamic-update-slice_fusion.5
  42.0 1.3 convolution_subtract_fusion.11
  43.3 11.7 %cholesky.305 = f32[128,128]{1,0:T(8,128)S(1)} custom-call(f32[128,128]{1,0:T(8,128)S(1)} %cholesky.430), custom_call_target="Cholesky" | custom-call | tf_op jit(solution)/shard_map/jit(cholesky)/cholesky | solution.py:52
  55.1 10.0 %custom-call.33 = f32[1,128,128]{1,2,0:T(8,128)S(1)} custom-call(f32[1,128,128]{2,1,0:T(8,128)S(1)} %get-tuple-element.78), custom_call_target="InvertDiagBlocksLowerTriangular" | custom-call | tf_op jit(solution)/shard_map/jit(cholesky)/cholesky | solution.py:52
  65.4 1.3 convolution_subtract_fusion.13
  66.7 11.7 %cholesky.326 = f32[128,128]{1,0:T(8,128)S(1)} custom-call(f32[128,128]{1,0:T(8,128)S(1)} %cholesky.435), custom_call_target="Cholesky" | custom-call | tf_op jit(solution)/shard_map/jit(cholesky)/cholesky | solution.py:52
  79.1 9.8 %custom-call.34 = f32[1,128,128]{1,2,0:T(8,128)S(1)} custom-call(f32[1,128,128]{2,1,0:T(8,128)S(1)} %get-tuple-element.75), custom_call_target="InvertDiagBlocksLowerTriangular" | custom-call | tf_op jit(solution)/shard_map/jit(cholesky)/cholesky | solution.py:52
  89.1 1.2 convolution_subtract_fusion.15
  90.3 22.2 %cholesky.343 = f32[128,128]{1,0:T(8,128)S(1)} custom-call(f32[128,128]{1,0:T(8,128)S(1)} %convolution_subtract_fusion.15), custom_call_target="Cholesky" | custom-call | tf_op jit(solution)/shard_map/jit(cholesky)/cholesky | solution.py:52
  112.5 0.7 compare_reduce_fusion.4
  116.4 1.1 select_select_fusion.1
  117.5 0.7 broadcast.236.clone
  118.3 13.7 %while.5 = (s32[]{:T(128)}, f32[512,512]{1,0:T(8,128)}, s32[4,2]{0,1:T(2,128)S(1)}, f32[4,128,128]{2,1,0:T(8,128)}, s32[]{:T(128)}) while((s32[]{:T(128)}, f32[512,512]{1,0:T(8,128)}, s32[4,2]{0,1:T(2,128)S(1)}, f32[4,128,128]{2,1,0:T(8,128)}, s32[]{:T(128)}) %tuple.68), condition=%wide.while_cond, body=%wide.while_body.sunk | while | flops 2 | bytes 132205 | solution.py:15
  118.9 2.8 bitcast_dynamic-update-slice_fusion.4
  122.3 2.8 bitcast_dynamic-update-slice_fusion.4
  125.8 2.8 bitcast_dynamic-update-slice_fusion.4
  129.2 2.7 bitcast_dynamic-update-slice_fusion.4
  132.0 40.2 %custom-call.35 = f32[4,128,128]{1,2,0:T(8,128)S(1)} custom-call(f32[4,128,128]{2,1,0:T(8,128)} %get-tuple-element.26), custom_call_target="InvertDiagBlocksLowerTriangular" | custom-call | tf_op jit(solution)/shard_map/jit(_solve_triangular)/triangular_solve | solution.py:15
  172.2 1.5 fusion.105
  173.7 1.4 convolution_subtract_fusion.8
  177.6 1.5 convolution_subtract_fusion
  179.0 1.6 copy.34
  180.9 1.0 copy-done.5
  181.9 11.7 %cholesky.358 = f32[128,128]{1,0:T(8,128)S(1)} custom-call(f32[128,128]{1,0:T(8,128)S(1)} %cholesky.439), custom_call_target="Cholesky" | custom-call | tf_op jit(solution)/shard_map/jit(cholesky)/cholesky | solution.py:55
  193.6 9.8 %custom-call.36 = f32[1,128,128]{1,2,0:T(8,128)S(1)} custom-call(f32[1,128,128]{2,1,0:T(8,128)S(1)} %get-tuple-element.71), custom_call_target="InvertDiagBlocksLowerTriangular" | custom-call | tf_op jit(solution)/shard_map/jit(cholesky)/cholesky | solution.py:55
  203.6 1.2 constant_dynamic-update-slice_fusion.3
  204.8 1.3 convolution_subtract_fusion.10
  206.1 12.1 %cholesky.377 = f32[128,128]{1,0:T(8,128)S(1)} custom-call(f32[128,128]{1,0:T(8,128)S(1)} %cholesky.443), custom_call_target="Cholesky" | custom-call | tf_op jit(solution)/shard_map/jit(cholesky)/cholesky | solution.py:55
  218.2 9.8 %custom-call.37 = f32[1,128,128]{1,2,0:T(8,128)S(1)} custom-call(f32[1,128,128]{2,1,0:T(8,128)S(1)} %get-tuple-element.68), custom_call_target="InvertDiagBlocksLowerTriangular" | custom-call | tf_op jit(solution)/shard_map/jit(cholesky)/cholesky | solution.py:55
  228.3 1.3 convolution_subtract_fusion.12
  229.6 11.7 %cholesky.398 = f32[128,128]{1,0:T(8,128)S(1)} custom-call(f32[128,128]{1,0:T(8,128)S(1)} %cholesky.448), custom_call_target="Cholesky" | custom-call | tf_op jit(solution)/shard_map/jit(cholesky)/cholesky | solution.py:55
  241.4 9.8 %custom-call.38 = f32[1,128,128]{1,2,0:T(8,128)S(1)} custom-call(f32[1,128,128]{2,1,0:T(8,128)S(1)} %get-tuple-element.65), custom_call_target="InvertDiagBlocksLowerTriangular" | custom-call | tf_op jit(solution)/shard_map/jit(cholesky)/cholesky | solution.py:55
  251.4 1.2 convolution_subtract_fusion.14
  252.6 11.7 %cholesky.415 = f32[128,128]{1,0:T(8,128)S(1)} custom-call(f32[128,128]{1,0:T(8,128)S(1)} %convolution_subtract_fusion.14), custom_call_target="Cholesky" | custom-call | tf_op jit(solution)/shard_map/jit(cholesky)/cholesky | solution.py:55
  265.0 0.7 compare_reduce_fusion.2
  269.6 8.1 %while.6 = (s32[]{:T(128)}, f32[512,512]{1,0:T(8,128)S(1)}, s32[4,2]{0,1:T(2,128)S(1)}, f32[4,128,128]{2,1,0:T(8,128)S(1)}, s32[]{:T(128)}) while((s32[]{:T(128)}, f32[512,512]{1,0:T(8,128)S(1)}, s32[4,2]{0,1:T(2,128)S(1)}, f32[4,128,128]{2,1,0:T(8,128)S(1)}, s32[]{:T(128)}) %tuple.78), condition=%wide.while_cond.clone, body=%wide.while_body.clone.sunk | while | flops 2 | bytes 131189 | solution.py:15
  270.2 1.3 bitcast_dynamic-update-slice_fusion.5
  272.3 1.3 bitcast_dynamic-update-slice_fusion.5
  274.3 1.3 bitcast_dynamic-update-slice_fusion.5
  276.3 1.3 bitcast_dynamic-update-slice_fusion.5
  277.7 39.9 %custom-call.39 = f32[4,128,128]{1,2,0:T(8,128)} custom-call(f32[4,128,128]{2,1,0:T(8,128)S(1)} %get-tuple-element.27), custom_call_target="InvertDiagBlocksLowerTriangular" | custom-call | tf_op jit(solution)/shard_map/jit(_solve_triangular)/triangular_solve | solution.py:15
  317.6 5.4 %fusion.102 = (bf16[1,768,512]{2,0,1:T(2,128)(2,1)S(1)}, bf16[1,768,512]{2,0,1:T(2,128)(2,1)}) fusion(bf16[2,768,512]{2,0,1:T(2,128)(2,1)} %all-gather.2.cloned.1.call-done), kind=kLoop, calls=%fused_computation.197 | loop fusion | bytes 3145728 | tf_op jit(solution)/shard_map/slice | solution.py:57
  323.0 1.5 copy.44
  324.7 0.8 copy-done.9
  328.2 0.9 convolution_subtract_fusion.3
  329.7 1.3 copy-done.6
  332.5 1.6 convolution_subtract_fusion.2
  334.7 2.3 convolution_subtract_fusion.5
  337.6 3.1 convolution_subtract_fusion.1
  341.3 1.3 fusion
  343.0 0.9 copy.39
  343.9 63.7 %all-reduce.3.cloned.1.call-done = bf16[2,768,512]{1,2,0:T(8,128)(2,1)} async-done(((bf16[2,768,512]{1,2,0:T(8,128)(2,1)}), bf16[2,768,512]{1,2,0:T(8,128)(2,1)}) %all-reduce.3.cloned.1.call-update) | async-done | bytes 1572880 | tf_op jit(solution)/shard_map/psum | solution.py:11
  407.6 1.5 slice_bitcast_fusion.3
  409.1 2.5 subtract_convert_fusion
  (118 shorter events, 22.3 us)
Async XLA Ops:
  7.2 310.5 %all-gather.2.cloned.1.call-start = ((), (), s32[]{:S(2)}) async-start(), calls=%async_computation | async-start | bytes 1966080 | tf_op jit(solution)/shard_map/all_gather | solution.py:56
  10.6 1.3 copy-start.10
  11.9 395.7 %all-reduce.3.cloned.1.call-start = ((), (), s32[]{:S(2)}) async-start(), calls=%async_computation.1 | async-start | bytes 3145728 | tf_op jit(solution)/shard_map/psum | solution.py:11
  12.7 1.6 copy-start.7
  18.1 1.0 copy-start.4
  132.0 43.6 %copy-start = (f32[512,512]{1,0:T(8,128)S(1)}, f32[512,512]{1,0:T(8,128)}, u32[]{:S(2)}) copy-start(f32[512,512]{1,0:T(8,128)} %get-tuple-element.187) | copy-start | bytes 3145732
  172.2 4.9 %copy-start.8 = (f32[4,128,128]{1,2,0:T(8,128)}, f32[4,128,128]{1,2,0:T(8,128)S(1)}, u32[]{:S(2)}) copy-start(f32[4,128,128]{1,2,0:T(8,128)S(1)} %custom-call.35) | copy-start | bytes 786436
  172.2 3.4 copy-start.2
  173.7 3.8 copy-start.12
  175.5 2.0 copy-start.14
  176.4 1.1 copy-start.16
  179.0 1.7 copy-start.1
  180.9 1.0 copy-start.5
  277.7 39.9 %copy-start.3 = (f32[512,512]{1,0:T(8,128)}, f32[512,512]{1,0:T(8,128)S(1)}, u32[]{:S(2)}) copy-start(f32[512,512]{1,0:T(8,128)S(1)} %get-tuple-element.188) | copy-start | bytes 3145732
  324.6 1.0 copy-start.9
  329.6 1.4 copy-start.6
  329.6 1.4 copy-start.13
  329.6 1.4 copy-start.15
  329.6 1.4 copy-start.17
  331.0 0.9 copy-start.11
  343.9 65.1 %copy-start.18 = (bf16[768,768]{1,0:T(8,128)(2,1)S(1)}, bf16[768,768]{1,0:T(8,128)(2,1)}, u32[]{:S(2)}) copy-start(bf16[768,768]{1,0:T(8,128)(2,1)} %param.10) | copy-start | bytes 3538948
Sparse Core Ops, SparseCore 0:
  12.0 33.8 all-gather.1
  342.7 64.7 all-reduce.2
where the time goes:
time: 424 us; the launch traced here: 419 us
  other arithmetic  256 us (60%)
  waiting for transfers between devices  63.7 us (15%)
  local copies, waits for them, and re-layouts  44.5 us (10%)
  matrix products  33.8 us (8%)
  between operations  20.5 us (5%)
    another operation x14, other arithmetic, local(): first_factor = jnp.linalg.cholesky(diagonals[0])  89.2 us
    another operation x5, other arithmetic, solve_right(): return jax.scipy.linalg.solve_triangular(lower_factor, rhs.T, lower=True).T  81.4 us
    another operation x15, other arithmetic, local(): second_factor = jnp.linalg.cholesky(shrunk)  79.4 us
    psum x1, waiting for transfers between devices, from_root(): return lax.psum(kept, axis)  63.7 us
    another operation x27, local copies, waits for them, and re-layouts, solve_right(): return jax.scipy.linalg.solve_triangular(lower_factor, rhs.T, lower=True).T  22.5 us
    another operation x21, matrix products, solve_right(): return jax.scipy.linalg.solve_triangular(lower_factor, rhs.T, lower=True).T  18.3 us
    unnamed x43, local copies, waits for them, and re-layouts  9.28 us
  transfers between devices with their start and end apart: 2, of which 1 were waited for; matrix products, arithmetic and copies ran while one was open for 71% of the time, Pallas kernels for 0%

commit v1 on v0

--- a/solution.py
+++ b/solution.py
@@ -1,6 +1,10 @@
+import functools
+
 import jax
 import jax.numpy as jnp
 from jax import lax
+from jax.experimental import pallas as pl
+from jax.experimental.pallas import tpu as pltpu
 from jax.sharding import PartitionSpec as P
 
 B = 128
@@ -21,7 +25,7 @@
     )
 
 
-def local(
+def direct(
     trailing,
     offdiagonal_panel_rows,
     pivot_diagonal_blocks,
@@ -68,9 +72,333 @@
     return (result.astype(jnp.bfloat16), factor)
 
 
+CORES = 2
+MESH = pl.DeviceIdType.MESH
+TOLERANCE = 0.01
+F32 = jnp.float32
+BF16 = jnp.bfloat16
+
+
+def nt(left, right):
+    return lax.dot_general(left, right, (((1,), (1,)), ((), ())), preferred_element_type=F32)
+
+
+def nn(left, right):
+    return lax.dot_general(left, right, (((1,), (0,)), ((), ())), preferred_element_type=F32)
+
+
+def split(value):
+    high = value.astype(BF16)
+    return high, (value - high.astype(F32)).astype(BF16)
+
+
+def tiles(order):
+    step = 256 if order % 256 == 0 else order
+    return [(start, step) for start in range(0, order, step)]
+
+
+def places(start, rows, columns):
+    row = start + lax.broadcasted_iota(jnp.int32, (rows, columns), 0)
+    column = lax.broadcasted_iota(jnp.int32, (rows, columns), 1)
+    return row, column
+
+
+def lower_half(value, start):
+    row, column = places(start, *value.shape)
+    return jnp.where(column < row, value, jnp.where(column == row, 0.5 * value, 0.0))
+
+
+def less_identity(value, start):
+    row, column = places(start, *value.shape)
+    return value - jnp.where(row == column, 1.0, 0.0)
+
+
+def correct(f_ref, x_ref, order):
+    for start, rows in tiles(order):
+        part = pl.ds(start, rows)
+        f = f_ref[part, :]
+        square = nt(f, f_ref[...])
+        x_ref[part, :] = (f.astype(F32) - lower_half(square, start)).astype(BF16)
+
+
+def open_inverse(a_ref, w_ref, f_ref, x_ref):
+    order = a_ref.shape[0]
+    a = a_ref[...].astype(F32)
+    row, column = places(0, order, order)
+    on_diagonal = jnp.where(row == column, a, 0.0)
+    down = lax.rsqrt(jnp.sum(on_diagonal, axis=1, keepdims=True))
+    across = lax.rsqrt(jnp.sum(on_diagonal, axis=0, keepdims=True))
+    f_ref[...] = jnp.where(column < row, a * down * across, 0.0).astype(BF16)
+    correct(f_ref, x_ref, order)
+    for start, rows in tiles(order):
+        part = pl.ds(start, rows)
+        x = x_ref[part, :]
+        square = nn(x, x_ref[...])
+        unit = -less_identity(jnp.zeros((rows, order), F32), start)
+        w_ref[part, :] = ((unit - x.astype(F32) + square) * across).astype(BF16)
+
+
+def cubic_inverse(a_ref, w_ref, f_ref, x_ref, y_ref):
+    order = a_ref.shape[0]
+    for start, rows in tiles(order):
+        part = pl.ds(start, rows)
+        image = nn(w_ref[part, :], a_ref[...]).astype(BF16)
+        error = less_identity(nt(image, w_ref[...]), start)
+        f_ref[part, :] = lower_half(error, start).astype(BF16)
+    correct(f_ref, x_ref, order)
+    for start, rows in tiles(order):
+        part = pl.ds(start, rows)
+        y_ref[part, :] = nn(x_ref[part, :], w_ref[...])
+    later = y_ref[...].astype(BF16)
+    for start, rows in tiles(order):
+        part = pl.ds(start, rows)
+        new = w_ref[part, :].astype(F32) - y_ref[part, :] + nn(x_ref[part, :], later)
+        w_ref[part, :] = new.astype(BF16)
+
+
+def close_inverse(a_ref, rest_ref, w_ref, f_ref, high_ref, low_ref):
+    order = a_ref.shape[0]
+    total = jnp.zeros((1, order), F32)
+    for start, rows in tiles(order):
+        part = pl.ds(start, rows)
+        image = nn(w_ref[part, :], a_ref[...])
+        if rest_ref is not None:
+            image = image + nn(w_ref[part, :], rest_ref[...])
+        high, low = split(image)
+        error = less_identity(nt(high, w_ref[...]) + nt(low, w_ref[...]), start)
+        f = lower_half(error, start)
+        total = total + jnp.sum(f * f, axis=0, keepdims=True)
+        f_ref[part, :] = f.astype(BF16)
+    for start, rows in tiles(order):
+        part = pl.ds(start, rows)
+        new = w_ref[part, :].astype(F32) - nn(f_ref[part, :], w_ref[...])
+        high, low = split(new)
+        high_ref[part, :] = high
+        if low_ref is not None:
+            low_ref[part, :] = low
+    return total
+
+
+def kernel(
+    col_count, row_count,
+    trailing_ref, panels_ref, diagonals_ref, coupling_ref, pattern_ref, lookup_ref, sequence_ref,
+    updated_ref, factor_ref, residual_ref,
+    row_rows, col_rows, a_ref, rest_ref, k_ref, w_ref, f_ref, x_ref, y_ref,
+    first_ref, low_ref, link_ref, second_ref, row_factor, col_factor, held,
+    row_send, row_recv, col_send, col_recv, held_sem,
+):
+    r = lax.axis_index("row")
+    c = lax.axis_index("col")
+    width, order = panels_ref.shape[1], panels_ref.shape[2]
+    z, source_z, last_z = r // CORES, c // CORES, row_count // CORES - 1
+    main = r % CORES == c % CORES
+    sibling = z * CORES + (CORES - 1 - r % CORES)
+    is_source = r == c
+    sends = (
+        (main & (z >= source_z) & (z < last_z), jnp.minimum(r + CORES, row_count - 1)),
+        (main & (z <= source_z) & (z > 0), jnp.maximum(r - CORES, 0)),
+        (main, sibling),
+    )
+
+    fetch = pltpu.make_async_copy(trailing_ref, held, held_sem)
+    fetch.start()
+
+    barrier = pltpu.get_barrier_semaphore()
+    for step in range(1, col_count):
+        pl.semaphore_signal(barrier, inc=1, device_id=(r, (c + step) % col_count), device_id_type=MESH)
+    pl.semaphore_signal(barrier, inc=1, device_id=(sibling, c), device_id_type=MESH)
+
+    @pl.when(z < last_z)
+    def _():
+        pl.semaphore_signal(barrier, inc=1, device_id=(r + CORES, c), device_id_type=MESH)
+
+    @pl.when(z > 0)
+    def _():
+        pl.semaphore_signal(barrier, inc=1, device_id=(r - CORES, c), device_id_type=MESH)
+
+    first_row = (r * col_count + c) * width
+    first_slot = first_row // B
+    slot_count = lookup_ref.shape[0]
+    slot_of_row = (first_row + lax.broadcasted_iota(jnp.int32, (width, order), 0)) // B
+    for panel in range(2):
+        which = sequence_ref[panel]
+        kept = jnp.zeros((width, order), jnp.int32)
+        for step in range((width + B - 2) // B + 1):
+            slot = jnp.minimum(first_slot + step, slot_count - 1)
+            flag = pattern_ref[which, lookup_ref[slot]]
+            kept = jnp.where(slot_of_row == first_slot + step, flag, kept)
+        values = panels_ref[which].astype(F32)
+        row_rows[c, panel] = jnp.where(kept == 1, values, 0.0).astype(BF16)
+
+    neighbours = col_count + (z < last_z).astype(jnp.int32) + (z > 0).astype(jnp.int32)
+    pl.semaphore_wait(barrier, neighbours)
+
+    def row_copy(step):
+        target = (r + step) % col_count
+        return target != c, pltpu.make_async_remote_copy(
+            src_ref=row_rows.at[c], dst_ref=row_rows.at[c],
+            send_sem=row_send.at[step], recv_sem=row_recv.at[c],
+            device_id=(r, target), device_id_type=MESH,
+        )
+
+    def row_wait(piece):
+        pltpu.make_async_remote_copy(
+            src_ref=row_rows.at[piece], dst_ref=row_rows.at[piece],
+            send_sem=row_send.at[0], recv_sem=row_recv.at[piece],
+            device_id=(r, c), device_id_type=MESH,
+        ).wait_recv()
+
+    def col_copy(step, panel, way, target):
+        piece = (c + step) % col_count
+        chunk = 2 * step + panel
+        return pltpu.make_async_remote_copy(
+            src_ref=col_rows.at[piece, panel], dst_ref=col_rows.at[piece, panel],
+            send_sem=col_send.at[way, chunk], recv_sem=col_recv.at[chunk],
+            device_id=(target, c), device_id_type=MESH,
+        )
+
+    for step in range(col_count):
+        wanted, copy = row_copy(step)
+        pl.when(wanted)(copy.start)
+
+    def forward(step, panel, arrived=False):
+        piece = (c + step) % col_count
+
+        @pl.when(is_source)
+        def _():
+            if step > 0 and panel == 0 and not arrived:
+                row_wait(piece)
+            col_rows[piece, panel] = row_rows[piece, panel]
+
+        @pl.when(jnp.logical_not(is_source))
+        def _():
+            col_copy(step, panel, 0, sibling).wait_recv()
+
+        for way, (wanted, target) in enumerate(sends):
+            pl.when(wanted)(col_copy(step, panel, way, target).start)
+
+    chunks = [(step, panel) for step in range(col_count) for panel in range(2)]
+    turn = iter(chunks)
+    share = -(-len(chunks) // 8)
+
+    def relay():
+        for _ in range(share):
+            chunk = next(turn, None)
+            if chunk is not None:
+                forward(*chunk)
+
+    a_ref[...] = diagonals_ref[sequence_ref[0]]
+    k = coupling_ref[...].astype(F32)
+    k_ref[...] = jnp.where(sequence_ref[0] == 1, k.T, k).astype(BF16)
+    open_inverse(a_ref, w_ref, f_ref, x_ref)
+    relay()
+    cubic_inverse(a_ref, w_ref, f_ref, x_ref, y_ref)
+    relay()
+    total = close_inverse(a_ref, None, w_ref, f_ref, first_ref, low_ref)
+    relay()
+    link_ref[...] = (nt(k_ref[...], first_ref[...]) + nt(k_ref[...], low_ref[...])).astype(BF16)
+    shrunk = diagonals_ref[sequence_ref[1]].astype(F32) - nt(link_ref[...], link_ref[...])
+    high, low = split(shrunk)
+    a_ref[...] = high
+    rest_ref[...] = low
+    open_inverse(a_ref, w_ref, f_ref, x_ref)
+    relay()
+    cubic_inverse(a_ref, w_ref, f_ref, x_ref, y_ref)
+    relay()
+    cubic_inverse(a_ref, w_ref, f_ref, x_ref, y_ref)
+    relay()
+    total = jnp.maximum(total, close_inverse(a_ref, rest_ref, w_ref, f_ref, second_ref, None))
+    relay()
+    residual_ref[...] = jnp.broadcast_to(jnp.sum(total, axis=1, keepdims=True), residual_ref.shape)
+
+    def factor_rows(rows, factors):
+        leading = nt(rows[0], first_ref[...]).astype(BF16)
+        factors[:, :order] = leading
+        rest = rows[1].astype(F32) - nt(leading, link_ref[...])
+        factors[:, order:] = nt(rest.astype(BF16), second_ref[...]).astype(BF16)
+
+    def pieces(ref):
+        return [ref[:, panel].reshape(col_count * width, order) for panel in range(2)]
+
+    left = list(turn)
+    late = [step for step, panel in left if panel == 0]
+    for step in range(1, col_count):
+        wait = functools.partial(row_wait, (c + step) % col_count)
+        if step in late:
+            wait()
+        else:
+            pl.when(jnp.logical_not(is_source))(wait)
+    factor_rows(pieces(row_rows), row_factor)
+    own = row_factor[pl.ds(pl.multiple_of(c * width, 16), width), :]
+    swapped = sequence_ref[0] == 1
+    mine = own[:, :order].astype(F32), own[:, order:].astype(F32)
+    factor_ref[0] = jnp.where(swapped, mine[1], mine[0]).astype(BF16)
+    factor_ref[1] = jnp.where(swapped, mine[0], mine[1]).astype(BF16)
+    for chunk in left:
+        forward(*chunk, arrived=True)
+    factor_rows(pieces(col_rows), col_factor)
+
+    fetch.wait()
+    height = held.shape[0]
+    for start in range(0, height, 256):
+        part = pl.ds(start, min(256, height - start))
+        change = nt(row_factor[part, :], col_factor[...])
+        updated_ref[part, :] = (held[part, :].astype(F32) - change).astype(BF16)
+
+    for step in range(col_count):
+        wanted, copy = row_copy(step)
+        pl.when(wanted)(copy.wait_send)
+    for step, panel in chunks:
+        for way, (wanted, target) in enumerate(sends):
+            pl.when(wanted)(col_copy(step, panel, way, target).wait_send)
+
+
+def local(col_count, row_count, trailing, panels, diagonals, coupling, pattern, lookup, sequence):
+    width, order = panels.shape[1], panels.shape[2]
+    rows, columns = trailing.shape
+    vmem = pl.BlockSpec(memory_space=pltpu.VMEM)
+    smem = pl.BlockSpec(memory_space=pltpu.SMEM)
+    square = (order, order)
+    rest = (trailing, panels, diagonals, coupling, pattern, lookup, sequence)
+    updated, factor, residual = pl.pallas_call(
+        functools.partial(kernel, col_count, row_count),
+        out_shape=(
+            jax.ShapeDtypeStruct(trailing.shape, BF16),
+            jax.ShapeDtypeStruct(panels.shape, BF16),
+            jax.ShapeDtypeStruct((8, 128), F32),
+        ),
+        in_specs=[pl.BlockSpec(memory_space=pl.ANY), vmem, vmem, vmem, smem, smem, smem],
+        out_specs=(vmem, vmem, vmem),
+        scratch_shapes=[
+            pltpu.VMEM((col_count, 2, width, order), BF16),
+            pltpu.VMEM((col_count, 2, width, order), BF16),
+            pltpu.VMEM(square, BF16), pltpu.VMEM(square, BF16), pltpu.VMEM(square, BF16),
+            pltpu.VMEM(square, BF16), pltpu.VMEM(square, BF16), pltpu.VMEM(square, BF16),
+            pltpu.VMEM(square, F32),
+            pltpu.VMEM(square, BF16), pltpu.VMEM(square, BF16), pltpu.VMEM(square, BF16),
+            pltpu.VMEM(square, BF16),
+            pltpu.VMEM((rows, 2 * order), BF16), pltpu.VMEM((columns, 2 * order), BF16),
+            pltpu.VMEM((rows, columns), BF16),
+            pltpu.SemaphoreType.DMA((col_count,)), pltpu.SemaphoreType.DMA((col_count,)),
+            pltpu.SemaphoreType.DMA((3, 2 * col_count)), pltpu.SemaphoreType.DMA((2 * col_count,)),
+            pltpu.SemaphoreType.DMA,
+        ],
+        compiler_params=pltpu.CompilerParams(
+            collective_id=0, has_side_effects=True, vmem_limit_bytes=48 * 2**20
+        ),
+        cost_estimate=pl.CostEstimate(flops=10**10, bytes_accessed=6 * 10**6, transcendentals=0),
+    )(*rest)
+    return lax.cond(
+        residual[0, 0] < TOLERANCE,
+        lambda *_: (updated, factor),
+        lambda *args: direct(*args),
+        *rest,
+    )
+
+
 def solution(mesh):
     return jax.shard_map(
-        local,
+        functools.partial(local, mesh.shape["col"], mesh.shape["row"]),
         mesh=mesh,
         in_specs=(P("row", "col"), P(None, ("row", "col"), None), P(), P(), P(), P(), P()),
         out_specs=(P("row", "col"), P(None, ("row", "col"), None)),

time: 424 us -> 65.7 us (0.15)
  the two profiles are of different devices: /device:TPU:0 before, /device:TPU:25 now
where the time goes in v1:
time: 65.7 us; the launch traced here: 65.5 us
  Pallas kernels  46.8 us (71%)
  between operations  14.8 us (23%)
  local copies, waits for them, and re-layouts  3.69 us (6%)
    pallas_call x1, Pallas kernels, local(): pl.pallas_call(functools.partial(kernel, col_count, row_count), out_shape...  46.8 us
    unnamed x14, local copies, waits for them, and re-layouts  3.18 us

profile of v1, /device:TPU:25, one launch (start us, length us, event | category | flops | bytes accessed | tf_op | source)
XLA Modules:
  0.0 65.5 jit_solution(15753466661521493380)
XLA Ops:
  7.2 0.0 copy-start.10
  7.2 0.0 copy-start.11
  7.2 0.0 copy-start.20
  7.2 0.0 copy-start.21
  7.2 0.0 copy-start.23
  7.2 46.8 %shard_map.90 = (bf16[768,768]{1,0:T(8,128)(2,1)}, bf16[2,192,512]{2,1,0:T(8,128)(2,1)}, f32[8,128]{1,0:T(8,128)S(1)}) custom-call(bf16[768,768]{1,0:T(8,128)(2,1)} %trailing_ref.1, bf16[2,192,512]{2,1,0:T(8,128)(2,1)} %panels_ref.1, bf16[2,512,512]{2,1,0:T(8,128)(2,1)} %diagonals_ref.1, bf16[512,512]{1,0:T(8,128)(2,1)} %coupling_ref.1, ...), custom_call_target="tpu_custom_call" | custom-call | flops 10000000000 | bytes 6000000 | tf_op jit(solution)/shard_map/pallas_call | solution.py:363
  54.0 0.5 slice.137
  55.1 0.0 copy-done.10
  55.2 0.0 copy-done.11
  55.2 0.0 copy-done.20
  55.2 0.0 copy-done.21
  55.2 0.0 copy-done.23
  55.2 0.3 conditional.1
  55.5 0.0 copy-start.12
  55.5 2.4 %copy.93 = bf16[768,768]{1,0:T(8,128)(2,1)} copy(bf16[768,768]{1,0:T(8,128)(2,1)} %get-tuple-element.251) | data formatting | bytes 2359296
  57.9 0.0 copy-done.12
  57.9 0.7 %copy.94 = bf16[2,192,512]{2,1,0:T(8,128)(2,1)} copy(bf16[2,192,512]{2,1,0:T(8,128)(2,1)S(1)} %copy-done.12) | data formatting | bytes 786432
Async XLA Ops:
  7.2 48.0 %copy-start.10 = (bf16[512,512]{1,0:T(8,128)(2,1)S(1)}, bf16[512,512]{1,0:T(8,128)(2,1)}, u32[]{:S(2)}) copy-start(bf16[512,512]{1,0:T(8,128)(2,1)} %coupling_ref.1) | copy-start | bytes 1572868
  7.2 48.0 %copy-start.11 = (bf16[2,192,512]{2,1,0:T(8,128)(2,1)S(1)}, bf16[2,192,512]{2,1,0:T(8,128)(2,1)}, u32[]{:S(2)}) copy-start(bf16[2,192,512]{2,1,0:T(8,128)(2,1)} %panels_ref.1) | copy-start | bytes 1179652
  7.2 48.0 %copy-start.20 = (s32[2,48]{1,0:T(2,128)S(1)}, s32[2,48]{1,0:T(2,128)}, u32[]{:S(2)}) copy-start(s32[2,48]{1,0:T(2,128)} %pattern_ref.1) | copy-start | bytes 1156
  7.2 48.0 %copy-start.21 = (s32[48]{0:T(128)S(1)}, s32[48]{0:T(128)}, u32[]{:S(2)}) copy-start(s32[48]{0:T(128)} %lookup_ref.1) | copy-start | bytes 580
  7.2 48.0 %copy-start.23 = (s32[2]{0:T(128)S(1)}, s32[2]{0:T(128)}, u32[]{:S(2)}) copy-start(s32[2]{0:T(128)} %sequence_ref.1) | copy-start | bytes 28
  55.5 2.4 %copy-start.12 = (bf16[2,192,512]{2,1,0:T(8,128)(2,1)S(1)}, bf16[2,192,512]{2,1,0:T(8,128)(2,1)}, u32[]{:S(2)}) copy-start(bf16[2,192,512]{2,1,0:T(8,128)(2,1)} %get-tuple-element.252) | copy-start | bytes 1179652

commit v2 on v1

v2 whole, which is shorter than its diff:
```python
import functools

import jax
import jax.numpy as jnp
from jax import lax
from jax.experimental import pallas as pl
from jax.experimental.pallas import tpu as pltpu
from jax.sharding import PartitionSpec as P

B = 128
CORES = 2
MESH = pl.DeviceIdType.MESH
TOLERANCE = 0.01
F32 = jnp.float32
BF16 = jnp.bfloat16


def nt(left, right):
    return lax.dot_general(left, right, (((1,), (1,)), ((), ())), preferred_element_type=F32)


def nn(left, right):
    return lax.dot_general(left, right, (((1,), (0,)), ((), ())), preferred_element_type=F32)


def split(value):
    high = value.astype(BF16)
    return high, (value - high.astype(F32)).astype(BF16)


def blocks(order):
    size = 256 if order % 256 == 0 else order
    return size, order // size


def place(index, size):
    return pl.ds(index * size, size)


def ramp(index, size):
    return pl.ds(0, (index + 1) * size)


def on_diagonal(size):
    row = lax.broadcasted_iota(jnp.int32, (size, size), 0)
    column = lax.broadcasted_iota(jnp.int32, (size, size), 1)
    return row, column


def lower_half(value, i, j):
    if j < i:
        return value
    row, column = on_diagonal(value.shape[0])
    return jnp.where(column < row, value, jnp.where(column == row, 0.5 * value, 0.0))


def less_identity(value, i, j):
    if j < i:
        return value
    row, column = on_diagonal(value.shape[0])
    return value - jnp.where(row == column, 1.0, 0.0)


def correct(f_ref, x_ref, tick):
    size, count = blocks(f_ref.shape[0])
    for i in range(count):
        for j in range(i + 1):
            square = nt(f_ref[place(i, size), ramp(j, size)], f_ref[place(j, size), ramp(j, size)])
            f = f_ref[place(i, size), place(j, size)].astype(F32)
            x_ref[place(i, size), place(j, size)] = (f - lower_half(square, i, j)).astype(BF16)
        tick()


def lower_product(x_ref, y_ref, i, j, size):
    middle = pl.ds(j * size, (i - j + 1) * size)
    return nn(x_ref[place(i, size), middle], y_ref[middle, place(j, size)])


def open_inverse(a_ref, w_ref, f_ref, x_ref, tick):
    size, count = blocks(a_ref.shape[0])
    row, column = on_diagonal(size)
    across = []
    for i in range(count):
        a = a_ref[place(i, size), place(i, size)].astype(F32)
        diagonal = jnp.where(row == column, a, 0.0)
        down = lax.rsqrt(jnp.sum(diagonal, axis=1, keepdims=True))
        across.append(lax.rsqrt(jnp.sum(diagonal, axis=0, keepdims=True)))
        for j in range(i + 1):
            f = a_ref[place(i, size), place(j, size)].astype(F32) * down * across[j]
            if i == j:
                f = jnp.where(column < row, f, 0.0)
            f_ref[place(i, size), place(j, size)] = f.astype(BF16)
    correct(f_ref, x_ref, tick)
    for i in range(count):
        for j in range(i + 1):
            x = x_ref[place(i, size), place(j, size)].astype(F32)
            new = lower_product(x_ref, x_ref, i, j, size) - x
            if i == j:
                new = new + jnp.where(row == column, 1.0, 0.0)
            w_ref[place(i, size), place(j, size)] = (new * across[j]).astype(BF16)
        tick()


def cubic_inverse(a_ref, w_ref, f_ref, x_ref, y_ref, tick):
    size, count = blocks(a_ref.shape[0])
    for i in range(count):
        own = ramp(i, size)
        image = nn(w_ref[place(i, size), own], a_ref[own, own]).astype(BF16)
        for j in range(i + 1):
            square = nt(image[:, : (j + 1) * size], w_ref[place(j, size), ramp(j, size)])
            f = lower_half(less_identity(square, i, j), i, j)
            f_ref[place(i, size), place(j, size)] = f.astype(BF16)
        tick()
    correct(f_ref, x_ref, tick)
    for i in range(count):
        for j in range(i + 1):
            y_ref[place(i, size), place(j, size)] = lower_product(x_ref, w_ref, i, j, size).astype(BF16)
        tick()
    for i in range(count):
        for j in range(i + 1):
            spot = place(i, size), place(j, size)
            change = lower_product(x_ref, y_ref, i, j, size) - y_ref[spot].astype(F32)
            w_ref[spot] = (w_ref[spot].astype(F32) + change).astype(BF16)
        tick()


def close_inverse(a_ref, rest_ref, w_ref, f_ref, high_ref, low_ref, tick):
    size, count = blocks(a_ref.shape[0])
    total = jnp.zeros((1, size), F32)
    for i in range(count):
        own = ramp(i, size)
        image = nn(w_ref[place(i, size), own], a_ref[own, own])
        if rest_ref is not None:
            image = image + nn(w_ref[place(i, size), own], rest_ref[own, own])
        high, low = split(image)
        for j in range(i + 1):
            far = (j + 1) * size
            beside = w_ref[place(j, size), ramp(j, size)]
            square = nt(high[:, :far], beside) + nt(low[:, :far], beside)
            f = lower_half(less_identity(square, i, j), i, j)
            total = total + jnp.sum(f * f, axis=0, keepdims=True)
            f_ref[place(i, size), place(j, size)] = f.astype(BF16)
        tick()
    for i in range(count):
        for j in range(i + 1):
            spot = place(i, size), place(j, size)
            new = w_ref[spot].astype(F32) - lower_product(f_ref, w_ref, i, j, size)
            high_ref[spot], low_ref[spot] = split(new)
        tick()
    return total


def solved(high, high_ref, low_ref, low=None):
    size, count = blocks(high_ref.shape[0])
    parts = []
    for j in range(count):
        far = (j + 1) * size
        beside = high_ref[place(j, size), ramp(j, size)]
        part = nt(high[:, :far], beside) + nt(high[:, :far], low_ref[place(j, size), ramp(j, size)])
        if low is not None:
            part = part + nt(low[:, :far], beside)
        parts.append(part)
    return jnp.concatenate(parts, axis=1) if count > 1 else parts[0]


def lead(rows, factors, first_ref, low_ref):
    order = first_ref.shape[0]
    factors[:, :order] = solved(rows[0], first_ref, low_ref).astype(BF16)


def follow(rows, factors, link_ref, second_ref, rest_ref):
    order = link_ref.shape[0]
    rest = rows[1].astype(F32) - nt(factors[:, :order], link_ref[...])
    high, low = split(rest)
    factors[:, order:] = solved(high, second_ref, rest_ref, low).astype(BF16)


def pieces(ref):
    count, _, width, order = ref.shape
    return [ref[:, panel].reshape(count * width, order) for panel in range(2)]


def write_factor(row_factor, factor_ref, sequence_ref, c):
    width, order = factor_ref.shape[1], factor_ref.shape[2]
    own = row_factor[pl.ds(pl.multiple_of(c * width, 16), width), :]
    swapped = sequence_ref[0] == 1
    mine = own[:, :order].astype(F32), own[:, order:].astype(F32)
    factor_ref[0] = jnp.where(swapped, mine[1], mine[0]).astype(BF16)
    factor_ref[1] = jnp.where(swapped, mine[0], mine[1]).astype(BF16)


def write_updated(row_factor, col_factor, held, updated_ref):
    height = held.shape[0]
    for start in range(0, height, 256):
        part = pl.ds(start, min(256, height - start))
        change = nt(row_factor[part, :], col_factor[...])
        updated_ref[part, :] = (held[part, :].astype(F32) - change).astype(BF16)


def eliminate(a_ref, w_ref, high_ref, low_ref):
    order = a_ref.shape[0]
    row = lax.broadcasted_iota(jnp.int32, (order, order), 0)
    column = lax.broadcasted_iota(jnp.int32, (order, order), 1)
    w_ref[...] = jnp.where(row == column, 1.0, 0.0)

    def step(j, carry):
        pivot_row = a_ref[pl.ds(j, 1), :]
        lane = lax.broadcasted_iota(jnp.int32, (1, order), 1)
        pivot = jnp.sum(jnp.where(lane == j, pivot_row, 0.0), axis=1, keepdims=True)
        scale = lax.rsqrt(pivot)
        pivot_row = pivot_row * scale
        done = w_ref[pl.ds(j, 1), :] * scale
        a = a_ref[...]
        below = jnp.sum(jnp.where(column == j, a, 0.0), axis=1, keepdims=True) * scale
        below = jnp.where(row[:, :1] > j, below, 0.0)
        a_ref[...] = a - below * pivot_row
        w_ref[...] = w_ref[...] - below * done
        w_ref[pl.ds(j, 1), :] = done
        return carry

    lax.fori_loop(0, order, step, 0)
    high_ref[...], low_ref[...] = split(w_ref[...])


def slow_kernel(
    trailing_ref, row_rows, col_rows, diagonals_ref, coupling_ref, sequence_ref,
    updated_ref, factor_ref,
    a_ref, w_ref, k_ref, first_ref, low_ref, link_ref, second_ref, rest_ref, row_factor, col_factor,
):
    a_ref[...] = diagonals_ref[sequence_ref[0]].astype(F32)
    k = coupling_ref[...].astype(F32)
    k_ref[...] = jnp.where(sequence_ref[0] == 1, k.T, k).astype(BF16)
    eliminate(a_ref, w_ref, first_ref, low_ref)
    link_ref[...] = solved(k_ref[...], first_ref, low_ref).astype(BF16)
    a_ref[...] = diagonals_ref[sequence_ref[1]].astype(F32) - nt(link_ref[...], link_ref[...])
    eliminate(a_ref, w_ref, second_ref, rest_ref)
    for rows, factors in ((row_rows, row_factor), (col_rows, col_factor)):
        lead(pieces(rows), factors, first_ref, low_ref)
        follow(pieces(rows), factors, link_ref, second_ref, rest_ref)
    write_factor(row_factor, factor_ref, sequence_ref, lax.axis_index("col"))
    write_updated(row_factor, col_factor, trailing_ref, updated_ref)


def kernel(
    col_count, row_count,
    trailing_ref, panels_ref, diagonals_ref, coupling_ref, pattern_ref, lookup_ref, sequence_ref,
    updated_ref, factor_ref, residual_ref, row_out, col_out,
    row_rows, col_rows, a_ref, rest_ref, k_ref, w_ref, f_ref, x_ref, y_ref,
    first_ref, low_ref, link_ref, second_ref, last_ref, row_factor, col_factor, held,
    row_send, row_recv, col_send, col_recv, held_sem, out_sem,
):
    r = lax.axis_index("row")
    c = lax.axis_index("col")
    width, order = panels_ref.shape[1], panels_ref.shape[2]
    z, source_z, last_z = r // CORES, c // CORES, row_count // CORES - 1
    main = r % CORES == c % CORES
    sibling = z * CORES + (CORES - 1 - r % CORES)
    is_source = r == c
    sends = (
        (main & (z >= source_z) & (z < last_z), jnp.minimum(r + CORES, row_count - 1)),
        (main & (z <= source_z) & (z > 0), jnp.maximum(r - CORES, 0)),
        (main, sibling),
    )

    fetch = pltpu.make_async_copy(trailing_ref, held, held_sem)
    fetch.start()

    barrier = pltpu.get_barrier_semaphore()
    for step in range(1, col_count):
        pl.semaphore_signal(barrier, inc=1, device_id=(r, (c + step) % col_count), device_id_type=MESH)
    pl.semaphore_signal(barrier, inc=1, device_id=(sibling, c), device_id_type=MESH)

    @pl.when(z < last_z)
    def _():
        pl.semaphore_signal(barrier, inc=1, device_id=(r + CORES, c), device_id_type=MESH)

    @pl.when(z > 0)
    def _():
        pl.semaphore_signal(barrier, inc=1, device_id=(r - CORES, c), device_id_type=MESH)

    first_row = (r * col_count + c) * width
    first_slot = first_row // B
    slot_count = lookup_ref.shape[0]
    slot_of_row = (first_row + lax.broadcasted_iota(jnp.int32, (width, order), 0)) // B
    for panel in range(2):
        which = sequence_ref[panel]
        kept = jnp.zeros((width, order), jnp.int32)
        for step in range((width + B - 2) // B + 1):
            slot = jnp.minimum(first_slot + step, slot_count - 1)
            flag = pattern_ref[which, lookup_ref[slot]]
            kept = jnp.where(slot_of_row == first_slot + step, flag, kept)
        values = panels_ref[which].astype(F32)
        row_rows[c, panel] = jnp.where(kept == 1, values, 0.0).astype(BF16)

    neighbours = col_count + (z < last_z).astype(jnp.int32) + (z > 0).astype(jnp.int32)
    pl.semaphore_wait(barrier, neighbours)

    def row_copy(step):
        target = (r + step) % col_count
        return target != c, pltpu.make_async_remote_copy(
            src_ref=row_rows.at[c], dst_ref=row_rows.at[c],
            send_sem=row_send.at[step], recv_sem=row_recv.at[c],
            device_id=(r, target), device_id_type=MESH,
        )

    def row_wait(piece):
        pltpu.make_async_remote_copy(
            src_ref=row_rows.at[piece], dst_ref=row_rows.at[piece],
            send_sem=row_send.at[0], recv_sem=row_recv.at[piece],
            device_id=(r, c), device_id_type=MESH,
        ).wait_recv()

    def col_copy(step, panel, way, target):
        piece = (c + step) % col_count
        chunk = 2 * step + panel
        return pltpu.make_async_remote_copy(
            src_ref=col_rows.at[piece, panel], dst_ref=col_rows.at[piece, panel],
            send_sem=col_send.at[way, chunk], recv_sem=col_recv.at[chunk],
            device_id=(target, c), device_id_type=MESH,
        )

    for step in range(col_count):
        wanted, copy = row_copy(step)
        pl.when(wanted)(copy.start)

    def forward(step, panel):
        piece = (c + step) % col_count

        @pl.when(is_source)
        def _():
            if step > 0 and panel == 0:
                row_wait(piece)
            col_rows[piece, panel] = row_rows[piece, panel]

        @pl.when(jnp.logical_not(is_source))
        def _():
            col_copy(step, panel, 0, sibling).wait_recv()

        for way, (wanted, target) in enumerate(sends):
            pl.when(wanted)(col_copy(step, panel, way, target).start)

    chunks = [(step, panel) for step in range(col_count) for panel in range(2)]
    turn = iter(chunks)
    ticks = iter(range(1, 1000))
    share = -(-len(chunks) // 8)

    def relay():
        if next(ticks) % 3 == 0:
            for _ in range(share):
                chunk = next(turn, None)
                if chunk is not None:
                    pl.when(main)(functools.partial(forward, *chunk))

    a_ref[...] = diagonals_ref[sequence_ref[0]]
    k = coupling_ref[...].astype(F32)
    k_ref[...] = jnp.where(sequence_ref[0] == 1, k.T, k).astype(BF16)
    open_inverse(a_ref, w_ref, f_ref, x_ref, relay)
    cubic_inverse(a_ref, w_ref, f_ref, x_ref, y_ref, relay)
    total = close_inverse(a_ref, None, w_ref, f_ref, first_ref, low_ref, relay)
    link_ref[...] = solved(k_ref[...], first_ref, low_ref).astype(BF16)
    relay()
    shrunk = diagonals_ref[sequence_ref[1]].astype(F32) - nt(link_ref[...], link_ref[...])
    a_ref[...], rest_ref[...] = split(shrunk)
    relay()
    open_inverse(a_ref, w_ref, f_ref, x_ref, relay)
    cubic_inverse(a_ref, w_ref, f_ref, x_ref, y_ref, relay)
    cubic_inverse(a_ref, w_ref, f_ref, x_ref, y_ref, relay)
    for chunk in turn:
        pl.when(main)(functools.partial(forward, *chunk))
    total = jnp.maximum(total, close_inverse(a_ref, rest_ref, w_ref, f_ref, second_ref, last_ref, lambda: None))
    residual_ref[...] = jnp.broadcast_to(jnp.sum(total, axis=1, keepdims=True), residual_ref.shape)

    for step in range(1, col_count):
        pl.when(jnp.logical_not(is_source))(functools.partial(row_wait, (c + step) % col_count))
    row_keep = pltpu.make_async_copy(row_rows, row_out, out_sem.at[0])
    row_keep.start()
    rows = pieces(row_rows)
    lead(rows, row_factor, first_ref, low_ref)
    follow(rows, row_factor, link_ref, second_ref, last_ref)
    write_factor(row_factor, factor_ref, sequence_ref, c)
    for chunk in chunks:
        pl.when(jnp.logical_not(main))(functools.partial(forward, *chunk))
    col_keep = pltpu.make_async_copy(col_rows, col_out, out_sem.at[1])
    col_keep.start()
    rows = pieces(col_rows)
    lead(rows, col_factor, first_ref, low_ref)
    follow(rows, col_factor, link_ref, second_ref, last_ref)

    fetch.wait()
    write_updated(row_factor, col_factor, held, updated_ref)
    row_keep.wait()
    col_keep.wait()
    for step in range(col_count):
        wanted, copy = row_copy(step)
        pl.when(wanted)(copy.wait_send)
    for step, panel in chunks:
        for way, (wanted, target) in enumerate(sends):
            pl.when(wanted)(col_copy(step, panel, way, target).wait_send)


def local(col_count, row_count, trailing, panels, diagonals, coupling, pattern, lookup, sequence):
    width, order = panels.shape[1], panels.shape[2]
    rows, columns = trailing.shape
    vmem = pl.BlockSpec(memory_space=pltpu.VMEM)
    smem = pl.BlockSpec(memory_space=pltpu.SMEM)
    square = (order, order)
    rest = (trailing, panels, diagonals, coupling, pattern, lookup, sequence)
    gathered = (col_count, 2, width, order)
    updated, factor, residual, row_rows, col_rows = pl.pallas_call(
        functools.partial(kernel, col_count, row_count),
        out_shape=(
            jax.ShapeDtypeStruct(trailing.shape, BF16),
            jax.ShapeDtypeStruct(panels.shape, BF16),
            jax.ShapeDtypeStruct((8, 128), F32),
            jax.ShapeDtypeStruct(gathered, BF16),
            jax.ShapeDtypeStruct(gathered, BF16),
        ),
        in_specs=[pl.BlockSpec(memory_space=pl.ANY), vmem, vmem, vmem, smem, smem, smem],
        out_specs=(vmem, vmem, vmem, pl.BlockSpec(memory_space=pl.ANY), pl.BlockSpec(memory_space=pl.ANY)),
        scratch_shapes=[
            pltpu.VMEM((col_count, 2, width, order), BF16),
            pltpu.VMEM((col_count, 2, width, order), BF16),
            pltpu.VMEM(square, BF16), pltpu.VMEM(square, BF16), pltpu.VMEM(square, BF16),
            pltpu.VMEM(square, BF16), pltpu.VMEM(square, BF16), pltpu.VMEM(square, BF16),
            pltpu.VMEM(square, BF16),
            pltpu.VMEM(square, BF16), pltpu.VMEM(square, BF16), pltpu.VMEM(square, BF16),
            pltpu.VMEM(square, BF16), pltpu.VMEM(square, BF16),
            pltpu.VMEM((rows, 2 * order), BF16), pltpu.VMEM((columns, 2 * order), BF16),
            pltpu.VMEM((rows, columns), BF16),
            pltpu.SemaphoreType.DMA((col_count,)), pltpu.SemaphoreType.DMA((col_count,)),
            pltpu.SemaphoreType.DMA((3, 2 * col_count)), pltpu.SemaphoreType.DMA((2 * col_count,)),
            pltpu.SemaphoreType.DMA, pltpu.SemaphoreType.DMA((2,)),
        ],
        compiler_params=pltpu.CompilerParams(
            collective_id=0, has_side_effects=True, vmem_limit_bytes=48 * 2**20
        ),
        cost_estimate=pl.CostEstimate(flops=10**10, bytes_accessed=6 * 10**6, transcendentals=0),
    )(*rest)
    slow = pl.pallas_call(
        slow_kernel,
        out_shape=(
            jax.ShapeDtypeStruct(trailing.shape, BF16),
            jax.ShapeDtypeStruct(panels.shape, BF16),
        ),
        in_specs=[vmem, vmem, vmem, vmem, vmem, smem],
        out_specs=(vmem, vmem),
        scratch_shapes=[pltpu.VMEM(square, F32), pltpu.VMEM(square, F32)]
        + [pltpu.VMEM(square, BF16)] * 6
        + [pltpu.VMEM((rows, 2 * order), BF16), pltpu.VMEM((columns, 2 * order), BF16)],
        compiler_params=pltpu.CompilerParams(vmem_limit_bytes=48 * 2**20),
    )
    return lax.cond(
        residual[0, 0] < TOLERANCE,
        lambda *_: (updated, factor),
        lambda *args: tuple(slow(*args)),
        trailing, row_rows, col_rows, diagonals, coupling, sequence,
    )


def solution(mesh):
    return jax.shard_map(
        functools.partial(local, mesh.shape["col"], mesh.shape["row"]),
        mesh=mesh,
        in_specs=(P("row", "col"), P(None, ("row", "col"), None), P(), P(), P(), P(), P()),
        out_specs=(P("row", "col"), P(None, ("row", "col"), None)),
        check_vma=False,
    )
```

time: 65.7 us -> 58 us (0.88)
  the two profiles are of different devices: /device:TPU:25 before, /device:TPU:24 now
where the time goes in v2:
time: 58 us; the launch traced here: 57.8 us
  Pallas kernels  51.8 us (89%)
  local copies, waits for them, and re-layouts  4.61 us (8%)
  between operations  1.35 us (2%)
    pallas_call x1, Pallas kernels, local(): pl.pallas_call(functools.partial(kernel, col_count, row_count), out_shape...  51.8 us
    unnamed x16, local copies, waits for them, and re-layouts  4.1 us

profile of v2, /device:TPU:24, one launch (start us, length us, event | category | flops | bytes accessed | tf_op | source)
XLA Modules:
  0.0 57.8 jit_solution(4477588650717561807)
XLA Ops:
  0.6 0.0 copy-start
  0.6 1.0 %copy-done = bf16[2,192,512]{2,1,0:T(8,128)(2,1)S(1)} copy-done((bf16[2,192,512]{2,1,0:T(8,128)(2,1)S(1)}, bf16[2,192,512]{2,1,0:T(8,128)(2,1)}, u32[]{:S(2)}) %copy-start) | copy-done | bytes 393240
  1.6 0.0 copy-start.1
  1.6 0.7 %copy-done.1 = s32[2,48]{1,0:T(2,128)S(1)} copy-done((s32[2,48]{1,0:T(2,128)S(1)}, s32[2,48]{1,0:T(2,128)}, u32[]{:S(2)}) %copy-start.1) | copy-done | bytes 408
  2.3 0.0 copy-start.2
  2.3 0.7 %copy-done.2 = s32[48]{0:T(128)S(1)} copy-done((s32[48]{0:T(128)S(1)}, s32[48]{0:T(128)}, u32[]{:S(2)}) %copy-start.2) | copy-done | bytes 216
  3.0 0.0 copy-start.3
  3.0 0.0 copy-start.4
  3.0 0.0 copy-start.5
  3.0 0.0 copy-start.6
  3.0 51.8 %shard_map.90 = (bf16[768,768]{1,0:T(8,128)(2,1)S(1)}, bf16[2,192,512]{2,1,0:T(8,128)(2,1)S(1)}, f32[8,128]{1,0:T(8,128)S(1)}, bf16[4,2,192,512]{3,2,1,0:T(8,128)(2,1)S(1)}, bf16[4,2,192,512]{3,2,1,0:T(8,128)(2,1)S(1)}) custom-call(bf16[768,768]{1,0:T(8,128)(2,1)} %trailing_ref.1, bf16[2,192,512]{2,1,0:T(8,128)(2,1)S(1)} %copy-done, ...), custom_call_target="tpu_custom_call" | custom-call | flops 10000000000 | bytes 6000000 | tf_op jit(solution)/shard_map/pallas_call | solution.py:409
  54.8 0.5 slice.3
  56.0 0.0 copy-done.3
  56.0 0.0 copy-done.4
  56.0 0.0 copy-done.5
  56.0 0.0 copy-done.6
  56.1 1.0 %copy.19 = bf16[768,768]{1,0:T(8,128)(2,1)} copy(bf16[768,768]{1,0:T(8,128)(2,1)S(1)} %get-tuple-element.46) | data formatting | bytes 2359296
  57.1 0.7 %copy.20 = bf16[2,192,512]{2,1,0:T(8,128)(2,1)} copy(bf16[2,192,512]{2,1,0:T(8,128)(2,1)S(1)} %get-tuple-element.47) | data formatting | bytes 786432
  (1 shorter events, 0.0 us)
Async XLA Ops:
  0.6 1.0 %copy-start = (bf16[2,192,512]{2,1,0:T(8,128)(2,1)S(1)}, bf16[2,192,512]{2,1,0:T(8,128)(2,1)}, u32[]{:S(2)}) copy-start(bf16[2,192,512]{2,1,0:T(8,128)(2,1)} %panels_ref.1) | copy-start | bytes 1179652
  1.6 0.7 %copy-start.1 = (s32[2,48]{1,0:T(2,128)S(1)}, s32[2,48]{1,0:T(2,128)}, u32[]{:S(2)}) copy-start(s32[2,48]{1,0:T(2,128)} %pattern_ref.1) | copy-start | bytes 1156
  2.3 0.7 %copy-start.2 = (s32[48]{0:T(128)S(1)}, s32[48]{0:T(128)}, u32[]{:S(2)}) copy-start(s32[48]{0:T(128)} %lookup_ref.1) | copy-start | bytes 580
  3.0 53.0 %copy-start.3 = (bf16[768,768]{1,0:T(8,128)(2,1)S(1)}, bf16[768,768]{1,0:T(8,128)(2,1)}, u32[]{:S(2)}) copy-start(bf16[768,768]{1,0:T(8,128)(2,1)} %trailing_ref.1) | copy-start | bytes 3538948
  3.0 53.0 %copy-start.4 = (bf16[2,512,512]{2,1,0:T(8,128)(2,1)S(1)}, bf16[2,512,512]{2,1,0:T(8,128)(2,1)}, u32[]{:S(2)}) copy-start(bf16[2,512,512]{2,1,0:T(8,128)(2,1)} %diagonals_ref.1) | copy-start | bytes 3145732
  3.0 53.0 %copy-start.5 = (bf16[512,512]{1,0:T(8,128)(2,1)S(1)}, bf16[512,512]{1,0:T(8,128)(2,1)}, u32[]{:S(2)}) copy-start(bf16[512,512]{1,0:T(8,128)(2,1)} %coupling_ref.1) | copy-start | bytes 1572868
  3.0 53.1 %copy-start.6 = (s32[2]{0:T(128)S(1)}, s32[2]{0:T(128)}, u32[]{:S(2)}) copy-start(s32[2]{0:T(128)} %sequence_ref.1) | copy-start | bytes 28

commit v3 on v2

--- a/solution.py
+++ b/solution.py
@@ -319,37 +319,50 @@
             device_id=(target, c), device_id_type=MESH,
         )
 
-    for step in range(col_count):
+    def send_row(step):
         wanted, copy = row_copy(step)
         pl.when(wanted)(copy.start)
 
-    def forward(step, panel):
+    send_row(0)
+
+    def forward(step, panel, from_source):
         piece = (c + step) % col_count
-
-        @pl.when(is_source)
-        def _():
+        if from_source:
             if step > 0 and panel == 0:
                 row_wait(piece)
             col_rows[piece, panel] = row_rows[piece, panel]
-
-        @pl.when(jnp.logical_not(is_source))
-        def _():
+        else:
             col_copy(step, panel, 0, sibling).wait_recv()
-
         for way, (wanted, target) in enumerate(sends):
             pl.when(wanted)(col_copy(step, panel, way, target).start)
 
     chunks = [(step, panel) for step in range(col_count) for panel in range(2)]
-    turn = iter(chunks)
+    share = -(-len(chunks) // 8)
+    groups = [chunks[start : start + share] for start in range(0, len(chunks), share)]
+    farthest = min(row_count // CORES - 1, 3)
+    away = jnp.minimum(jnp.abs(z - source_z), farthest)
+    plan = {distance: list(enumerate(groups)) for distance in range(farthest + 1)}
     ticks = iter(range(1, 1000))
-    share = -(-len(chunks) // 8)
+
+    def relay_group(distance, group):
+        @pl.when(main & (away == distance))
+        def _():
+            for step, panel in group:
+                forward(step, panel, distance == 0)
 
     def relay():
-        if next(ticks) % 3 == 0:
-            for _ in range(share):
-                chunk = next(turn, None)
-                if chunk is not None:
-                    pl.when(main)(functools.partial(forward, *chunk))
+        tick = next(ticks)
+        for distance, rest in plan.items():
+            if rest and tick == 3 + 3 * rest[0][0] + 5 * distance:
+                relay_group(distance, rest.pop(0)[1])
+        for step in range(1, col_count):
+            if tick == min(4 * step, 12):
+                send_row(step)
+
+    def finish_relays():
+        for distance, rest in plan.items():
+            while rest:
+                relay_group(distance, rest.pop(0)[1])
 
     a_ref[...] = diagonals_ref[sequence_ref[0]]
     k = coupling_ref[...].astype(F32)
@@ -365,9 +378,8 @@
     open_inverse(a_ref, w_ref, f_ref, x_ref, relay)
     cubic_inverse(a_ref, w_ref, f_ref, x_ref, y_ref, relay)
     cubic_inverse(a_ref, w_ref, f_ref, x_ref, y_ref, relay)
-    for chunk in turn:
-        pl.when(main)(functools.partial(forward, *chunk))
-    total = jnp.maximum(total, close_inverse(a_ref, rest_ref, w_ref, f_ref, second_ref, last_ref, lambda: None))
+    total = jnp.maximum(total, close_inverse(a_ref, rest_ref, w_ref, f_ref, second_ref, last_ref, relay))
+    finish_relays()
     residual_ref[...] = jnp.broadcast_to(jnp.sum(total, axis=1, keepdims=True), residual_ref.shape)
 
     for step in range(1, col_count):
@@ -378,13 +390,23 @@
     lead(rows, row_factor, first_ref, low_ref)
     follow(rows, row_factor, link_ref, second_ref, last_ref)
     write_factor(row_factor, factor_ref, sequence_ref, c)
-    for chunk in chunks:
-        pl.when(jnp.logical_not(main))(functools.partial(forward, *chunk))
+    for step in range(col_count):
+        piece = (c + step) % col_count
+
+        @pl.when(jnp.logical_not(main))
+        def _():
+            for panel in range(2):
+                col_copy(step, panel, 0, sibling).wait_recv()
+
+        here = pl.ds(pl.multiple_of(piece * width, 16), width)
+        rows = col_rows[piece, 0], col_rows[piece, 1]
+        leading = solved(rows[0], first_ref, low_ref).astype(BF16)
+        col_factor[here, :order] = leading
+        rest = rows[1].astype(F32) - nt(leading, link_ref[...])
+        high, low = split(rest)
+        col_factor[here, order:] = solved(high, second_ref, last_ref, low).astype(BF16)
     col_keep = pltpu.make_async_copy(col_rows, col_out, out_sem.at[1])
     col_keep.start()
-    rows = pieces(col_rows)
-    lead(rows, col_factor, first_ref, low_ref)
-    follow(rows, col_factor, link_ref, second_ref, last_ref)
 
     fetch.wait()
     write_updated(row_factor, col_factor, held, updated_ref)
@@ -432,7 +454,7 @@
             pltpu.SemaphoreType.DMA, pltpu.SemaphoreType.DMA((2,)),
         ],
         compiler_params=pltpu.CompilerParams(
-            collective_id=0, has_side_effects=True, vmem_limit_bytes=48 * 2**20
+            collective_id=0, has_side_effects=True, vmem_limit_bytes=60 * 2**20
         ),
         cost_estimate=pl.CostEstimate(flops=10**10, bytes_accessed=6 * 10**6, transcendentals=0),
     )(*rest)

time: 58 us -> 56.7 us (0.978)
  Pallas kernels: 51.8 us -> 50.6 us
    pallas_call x1, Pallas kernels: 51.8 us -> 50.6 us  [local(): pl.pallas_call(functools.partial(kernel, col_count, row_count), out_shape...]
    unnamed x16 -> x6, local copies, waits for them, and re-layouts: 4.1 us -> 3.11 us
    slice x1, local copies, waits for them, and re-layouts: 0.51 us -> 1.19 us  [local(): residual[0, 0] < TOLERANCE]
where the time goes in v3:
time: 56.7 us; the launch traced here: 56.5 us
  Pallas kernels  50.6 us (89%)
  local copies, waits for them, and re-layouts  4.3 us (8%)
  between operations  1.33 us (2%)
    pallas_call x1, Pallas kernels, local(): pl.pallas_call(functools.partial(kernel, col_count, row_count), out_shape...  50.6 us
    unnamed x6, local copies, waits for them, and re-layouts  3.11 us
    slice x1, local copies, waits for them, and re-layouts, local(): residual[0, 0] < TOLERANCE  1.19 us

profile of v3, /device:TPU:24, one launch (start us, length us, event | category | flops | bytes accessed | tf_op | source)
XLA Modules:
  0.0 56.5 jit_solution(4700517534334481142)
XLA Ops:
  0.6 0.0 copy-start.1
  0.6 0.0 copy-start
  0.7 50.6 %shard_map.90 = (bf16[768,768]{1,0:T(8,128)(2,1)}, bf16[2,192,512]{2,1,0:T(8,128)(2,1)S(1)}, f32[8,128]{1,0:T(8,128)}, bf16[4,2,192,512]{3,2,1,0:T(8,128)(2,1)S(1)}, bf16[4,2,192,512]{3,2,1,0:T(8,128)(2,1)S(1)}) custom-call(bf16[768,768]{1,0:T(8,128)(2,1)} %trailing_ref.1, bf16[2,192,512]{2,1,0:T(8,128)(2,1)} %panels_ref.1, ...), custom_call_target="tpu_custom_call" | custom-call | flops 10000000000 | bytes 6000000 | tf_op jit(solution)/shard_map/pallas_call | solution.py:431
  51.3 1.2 %slice.3 = f32[1,1]{1,0:T(1,128)} slice(f32[8,128]{1,0:T(8,128)} %get-tuple-element.29), slice={[0:1], [0:1]} | slice | bytes 8 | tf_op jit(solution)/shard_map/slice | solution.py:475
  53.1 0.0 copy-done.1
  53.1 0.0 copy-done
  53.2 0.2 conditional.1
  53.4 2.4 %copy.19 = bf16[768,768]{1,0:T(8,128)(2,1)} copy(bf16[768,768]{1,0:T(8,128)(2,1)} %get-tuple-element.46) | data formatting | bytes 2359296
  55.8 0.7 %copy.20 = bf16[2,192,512]{2,1,0:T(8,128)(2,1)} copy(bf16[2,192,512]{2,1,0:T(8,128)(2,1)S(1)} %get-tuple-element.47) | data formatting | bytes 786432
Async XLA Ops:
  0.6 52.5 %copy-start.1 = (s32[2]{0:T(128)S(1)}, s32[2]{0:T(128)}, u32[]{:S(2)}) copy-start(s32[2]{0:T(128)} %sequence_ref.1) | copy-start | bytes 28
  0.6 52.5 %copy-start = (bf16[512,512]{1,0:T(8,128)(2,1)S(1)}, bf16[512,512]{1,0:T(8,128)(2,1)}, u32[]{:S(2)}) copy-start(bf16[512,512]{1,0:T(8,128)(2,1)} %coupling_ref.1) | copy-start | bytes 1572868

commit v4 on v3

--- a/solution.py
+++ b/solution.py
@@ -324,6 +324,7 @@
         pl.when(wanted)(copy.start)
 
     send_row(0)
+    through = sends[0][0] | sends[1][0] | is_source
 
     def forward(step, panel, from_source):
         piece = (c + step) % col_count
@@ -345,7 +346,7 @@
     ticks = iter(range(1, 1000))
 
     def relay_group(distance, group):
-        @pl.when(main & (away == distance))
+        @pl.when(through & (away == distance))
         def _():
             for step, panel in group:
                 forward(step, panel, distance == 0)
@@ -377,7 +378,6 @@
     relay()
     open_inverse(a_ref, w_ref, f_ref, x_ref, relay)
     cubic_inverse(a_ref, w_ref, f_ref, x_ref, y_ref, relay)
-    cubic_inverse(a_ref, w_ref, f_ref, x_ref, y_ref, relay)
     total = jnp.maximum(total, close_inverse(a_ref, rest_ref, w_ref, f_ref, second_ref, last_ref, relay))
     finish_relays()
     residual_ref[...] = jnp.broadcast_to(jnp.sum(total, axis=1, keepdims=True), residual_ref.shape)
@@ -397,6 +397,11 @@
         def _():
             for panel in range(2):
                 col_copy(step, panel, 0, sibling).wait_recv()
+
+        @pl.when(main & jnp.logical_not(through))
+        def _():
+            for panel in range(2):
+                forward(step, panel, False)
 
         here = pl.ds(pl.multiple_of(piece * width, 16), width)
         rows = col_rows[piece, 0], col_rows[piece, 1]

time: 56.7 us -> 52.5 us (0.926)
  the two profiles are of different devices: /device:TPU:24 before, /device:TPU:19 now
where the time goes in v4:
time: 52.5 us; the launch traced here: 52.3 us
  Pallas kernels  46.4 us (88%)
  local copies, waits for them, and re-layouts  4.3 us (8%)
  between operations  1.33 us (3%)
    pallas_call x1, Pallas kernels, local(): pl.pallas_call(functools.partial(kernel, col_count, row_count), out_shape...  46.4 us
    unnamed x6, local copies, waits for them, and re-layouts  3.11 us
    slice x1, local copies, waits for them, and re-layouts, local(): residual[0, 0] < TOLERANCE  1.19 us

profile of v4, /device:TPU:19, one launch (start us, length us, event | category | flops | bytes accessed | tf_op | source)
XLA Modules:
  0.0 52.3 jit_solution(11477899134847880126)
XLA Ops:
  0.6 0.0 copy-start.1
  0.6 0.0 copy-start
  0.7 46.4 %shard_map.90 = (bf16[768,768]{1,0:T(8,128)(2,1)}, bf16[2,192,512]{2,1,0:T(8,128)(2,1)S(1)}, f32[8,128]{1,0:T(8,128)}, bf16[4,2,192,512]{3,2,1,0:T(8,128)(2,1)S(1)}, bf16[4,2,192,512]{3,2,1,0:T(8,128)(2,1)S(1)}) custom-call(bf16[768,768]{1,0:T(8,128)(2,1)} %trailing_ref.1, bf16[2,192,512]{2,1,0:T(8,128)(2,1)} %panels_ref.1, ...), custom_call_target="tpu_custom_call" | custom-call | flops 10000000000 | bytes 6000000 | tf_op jit(solution)/shard_map/pallas_call | solution.py:436
  47.1 1.2 %slice.3 = f32[1,1]{1,0:T(1,128)} slice(f32[8,128]{1,0:T(8,128)} %get-tuple-element.29), slice={[0:1], [0:1]} | slice | bytes 8 | tf_op jit(solution)/shard_map/slice | solution.py:480
  48.9 0.0 copy-done.1
  48.9 0.0 copy-done
  48.9 0.2 conditional.1
  49.2 2.4 %copy.19 = bf16[768,768]{1,0:T(8,128)(2,1)} copy(bf16[768,768]{1,0:T(8,128)(2,1)} %get-tuple-element.46) | data formatting | bytes 2359296
  51.5 0.7 %copy.20 = bf16[2,192,512]{2,1,0:T(8,128)(2,1)} copy(bf16[2,192,512]{2,1,0:T(8,128)(2,1)S(1)} %get-tuple-element.47) | data formatting | bytes 786432
Async XLA Ops:
  0.6 48.3 %copy-start.1 = (s32[2]{0:T(128)S(1)}, s32[2]{0:T(128)}, u32[]{:S(2)}) copy-start(s32[2]{0:T(128)} %sequence_ref.1) | copy-start | bytes 28
  0.6 48.3 %copy-start = (bf16[512,512]{1,0:T(8,128)(2,1)S(1)}, bf16[512,512]{1,0:T(8,128)(2,1)}, u32[]{:S(2)}) copy-start(bf16[512,512]{1,0:T(8,128)(2,1)} %coupling_ref.1) | copy-start | bytes 1572868
